TPU v7x, 32 devices: a whole 2x2x4 slice. The times are simulated.
32 devices in a mesh: leaf: 16 (over z, y, x), face: 2 (over core).
Axes of the slice: x: 2, y: 2, z: 4, core: 2. Of those that a mesh axis runs over, the one named last changes fastest.
Arguments:
- solve_ops: bfloat16 [32, 216, 384], P('leaf'), may hold values from -0.30618622 to 0.30618622, as said below
- inner_deriv: bfloat16 [6, 2, 32, 216], P(None, 'face'), may hold values from -1.796875 to 1.796875
- boundary_diag: float32 [6, 2, 32], P(None, 'face'), may hold values from 2.5 to 5
- wall_stencil: float32 [2, 32, 64], P('face'), may hold values from -0.3 to 0.3
- wall_coef: float32 [32, 6], P('leaf'), may hold values from 0.5 to 4
- cut_faces: int32 [32, 6], P('leaf'), may hold values 0 or 1
Outputs:
- merged: float32 [32, 4, 2, 32, 1024], P('leaf', None, 'face')
Inputs may be any that keep to these rules, and one draw needn't show every extreme that they name: `solve_ops`: entries of spread about 384 to the power -1/2.
All inputs are finite; a program needn't handle non-finite values. No bound on the sum of `cut_faces` on one device may be relied on, other than what follows from the above.
Results may differ from a plain program's by a relative error of at most 0.0003.
Values sent between devices are 32-bit elements; how exact they have to be, the bound alone decides.
A program may use at most 64 MiB of HBM per device.

v0:
```python
import jax
import jax.numpy as jnp
from jax import lax
from jax.sharding import PartitionSpec as P


def from_partner(shard, axis, apart):
    return lax.ppermute(shard, axis, [(i, i ^ 1 << apart) for i in range(lax.axis_size(axis))])


def solve_block(matrix, right):
    normal = jnp.einsum("lki,lkj->lij", matrix, matrix, precision=lax.Precision.HIGHEST)
    factor = jnp.linalg.cholesky(normal)
    projected = jnp.einsum("lki,lkj->lij", matrix, right, precision=lax.Precision.HIGHEST)
    return jax.scipy.linalg.cho_solve((factor, True), projected)


def pick_blocks(values, blocks, axis):
    return jnp.concatenate(
        [lax.slice_in_dim(values, index, index + 1, axis=axis) for index in blocks], axis=axis
    )


def split_columns(values, zero_box, axis):
    inner_set = (2, 7) if zero_box else (1, 6)
    outer_set = (0, 1, 3, 4, 5, 6, 8, 9) if zero_box else (0, 2, 3, 4, 5, 7, 8, 9)
    inner_part = pick_blocks(values, inner_set, axis)
    outer_part = pick_blocks(values, outer_set, axis)
    return (
        inner_part.reshape(inner_part.shape[:-2] + (-1,)),
        outer_part.reshape(outer_part.shape[:-2] + (-1,)),
    )


def local(solve_ops, inner_deriv, boundary_diag, wall_stencil, wall_coef, cut_faces):
    leaves, inner, bound = solve_ops.shape
    faces = inner_deriv.shape[0]
    half = inner_deriv.shape[2]
    width = bound // faces
    core = lax.axis_index("face")
    place = lax.axis_index("leaf")
    first = place % 2 == 0
    lower = place // 2 % 2 == 0
    rows = inner_deriv.reshape(faces * half, inner)
    dtn = jnp.einsum("ri,lic->lrc", rows, solve_ops, preferred_element_type=jnp.float32)
    dtn = dtn.reshape(leaves, faces, half, faces, width)
    same_face = jnp.eye(faces, dtype=jnp.float32)
    onehot = (jnp.arange(width)[None, :] == core * half + jnp.arange(half)[:, None]).astype(
        jnp.float32
    )
    dtn = dtn + jnp.einsum("fh,fg,hp->fhgp", boundary_diag[:, 0], same_face, onehot)[None]
    weights = cut_faces.astype(jnp.float32) * wall_coef
    dtn = (
        dtn
        + weights[:, :, None, None, None]
        * same_face[None, :, None, :, None]
        * wall_stencil[0][None, None, :, None, :]
    )
    own_inner = jnp.where(first, dtn[:, 1], dtn[:, 0])
    gathered = lax.all_gather(own_inner, "face", axis=1, tiled=True)
    sibling = from_partner(gathered, "leaf", 0)
    left_rows = jnp.where(first, gathered, sibling)
    right_rows = jnp.where(first, sibling, gathered)
    schur = left_rows[:, :, 1] + right_rows[:, :, 0]
    coupled = jnp.concatenate(
        [pick_blocks(left_rows, (0, 2, 3, 4, 5), 2), pick_blocks(right_rows, (1, 2, 3, 4, 5), 2)],
        axis=2,
    )
    coupled = coupled.reshape(leaves, width, 10 * width)
    solved = solve_block(schur, coupled)
    own_rows = jnp.where(first, pick_blocks(dtn, (0, 2, 3, 4, 5), 1), dtn[:, 1:6])
    own_outer = jnp.where(first, pick_blocks(own_rows, (0, 2, 3, 4, 5), 3), own_rows[:, :, :, 1:6])
    own_outer = own_outer.reshape(leaves, 5, half, 5 * width)
    own_face = jnp.where(first, own_rows[:, :, :, 1], own_rows[:, :, :, 0])
    blank = jnp.zeros_like(own_outer)
    diagonal_part = jnp.where(
        first,
        jnp.concatenate([own_outer, blank], axis=3),
        jnp.concatenate([blank, own_outer], axis=3),
    )
    level_one = diagonal_part - jnp.einsum(
        "lfhk,lkc->lfhc", own_face, solved, precision=lax.Precision.HIGHEST
    )
    box_face = jnp.where(lower, level_one[:, 2], level_one[:, 1])
    box_local = lax.all_gather(box_face, "face", axis=1, tiled=True)
    box_other = from_partner(box_local, "leaf", 0)
    box_inner = jnp.concatenate(
        [jnp.where(first, box_local, box_other), jnp.where(first, box_other, box_local)], axis=1
    )
    blocked = box_inner.reshape(leaves, 2 * width, 10, width)
    partner = from_partner(blocked, "leaf", 1)
    box_zero = jnp.where(lower, blocked, partner)
    box_one = jnp.where(lower, partner, blocked)
    zero_inner, zero_outer = split_columns(box_zero, True, 2)
    one_inner, one_outer = split_columns(box_one, False, 2)
    schur_two = zero_inner + one_inner
    solved_two = solve_block(schur_two, jnp.concatenate([zero_outer, one_outer], axis=2))
    kept = jnp.where(
        lower, pick_blocks(level_one, (0, 1, 3, 4), 1), pick_blocks(level_one, (0, 2, 3, 4), 1)
    )
    kept_blocks = kept.reshape(leaves, 4, half, 10, width)
    zero_keep_inner, zero_keep_outer = split_columns(kept_blocks, True, 3)
    one_keep_inner, one_keep_outer = split_columns(kept_blocks, False, 3)
    keep_inner = jnp.where(lower, zero_keep_inner, one_keep_inner)
    keep_outer = jnp.where(lower, zero_keep_outer, one_keep_outer)
    blank_two = jnp.zeros_like(keep_outer)
    diagonal_two = jnp.where(
        lower,
        jnp.concatenate([keep_outer, blank_two], axis=3),
        jnp.concatenate([blank_two, keep_outer], axis=3),
    )
    merged = diagonal_two - jnp.einsum(
        "lfhk,lkc->lfhc", keep_inner, solved_two, precision=lax.Precision.HIGHEST
    )
    return merged.reshape(leaves, 4, 1, half, 16 * width)


def solution(mesh):
    in_specs = (
        P("leaf", None, None),
        P(None, "face", None, None),
        P(None, "face", None),
        P("face", None, None),
        P("leaf", None),
        P("leaf", None),
    )
    out_specs = P("leaf", None, "face", None, None)
    return jax.shard_map(local, mesh=mesh, in_specs=in_specs, out_specs=out_specs, check_vma=False)
```

profile of v0, /device:TPU:1, one launch (start us, length us, event | category | flops | bytes accessed | tf_op | source)
XLA Modules:
  0.0 129.5 jit_solution(1113288619194894159)
XLA Ops:
  1.7 1.1 convolution_bitcast_fusion.1
  3.9 2.2 %all-gather = f32[2,1,64,6,64]{4,3,2,1,0:T(8,128)S(1)} all-gather(f32[2,1,32,6,64]{4,3,2,1,0:T(8,128)S(1)} %get-tuple-element.14), channel_id=2, replica_groups=mesh['leaf'=16,'face'=2] {'face'}, dimensions={2}, use_global_device_ids=true | all-gather | bytes 294912 | tf_op jit(solution)/shard_map/all_gather | solution.py:60
  6.1 2.3 %collective-permute-start = (f32[2,64,6,64]{3,2,1,0:T(8,128)S(1)}, f32[2,64,6,64]{3,2,1,0:T(8,128)}, u32[]{:S(2)}, u32[]{:S(2)}) collective-permute-start(f32[2,64,6,64]{3,2,1,0:T(8,128)S(1)} %bitcast.91), channel_id=1, source_target_pairs={{0,2},{2,0},{4,6},{6,4},{8,10},{10,8},{12,14},{14,12},{16,18},{18,... | collective-permute-start | bytes 589832 | tf_op jit(solution)/shard_map/ppermute | solution.py:8
  8.8 1.0 slice.252
  9.8 1.0 fusion.19
  10.8 1.6 %slice_select_fusion = f32[2,5,32,5,64]{4,3,2,1,0:T(8,128)S(1)} fusion(f32[2,5,32,6,64]{4,3,2,1,0:T(8,128)S(1)} %slice_select_fusion.1, f32[2,5,32,4,64]{4,3,2,1,0:T(4,128)} %slice.252, f32[2,5,32,1,64]{4,3,2,1,0:T(1,128)} %get-tuple-element.18, pred[]{:T(512)S(6)} %eq.32), kind=kLoop, calls=%fused_computation.5 | loop fusion | flops 204800 | bytes 1228801 | tf_op jit(solution)/shard_map/jit(_where)/select_n | solution.py:72
  12.4 1.0 reshape.99
  13.4 7.1 %collective-permute-done = f32[2,64,6,64]{3,2,1,0:T(8,128)} collective-permute-done((f32[2,64,6,64]{3,2,1,0:T(8,128)S(1)}, f32[2,64,6,64]{3,2,1,0:T(8,128)}, u32[]{:S(2)}, u32[]{:S(2)}) %collective-permute-start) | collective-permute-done | bytes 196640 | tf_op jit(solution)/shard_map/ppermute | solution.py:8
  20.6 1.1 broadcast_select_fusion.4
  22.4 11.7 %custom-call.22 = f32[2,64,64]{2,1,0:T(8,128)S(1)} custom-call(f32[2,64,64]{2,1,0:T(8,128)S(1)} %fusion.12), custom_call_target="Cholesky" | custom-call | tf_op jit(solution)/shard_map/jit(cholesky)/cholesky | solution.py:13
  34.4 9.8 %custom-call.23 = f32[2,1,64,64]{2,3,1,0:T(8,128)S(1)} custom-call(f32[2,1,64,64]{3,2,1,0:T(8,128)S(1)} %select_bitcast_fusion.1), custom_call_target="InvertDiagBlocksLowerTriangular" | custom-call | tf_op jit(solution)/shard_map/jit(_cho_solve)/vmap()/triangular_solve | solution.py:15
  44.9 0.9 fusion.26
  46.8 0.8 convolution_subtract_fusion.1
  47.7 0.9 concatenate.84
  48.7 1.5 %concatenate.85 = f32[2,3,32,10,64]{4,3,2,1,0:T(8,128)} reshape(f32[2,3,32,640]{3,2,1,0:T(8,128)S(1)} %slice.264) | data formatting | bytes 983040 | tf_op jit(solution)/shard_map/concatenate | solution.py:19
  50.4 1.2 concatenate.82
  51.6 2.7 %all-gather.1 = f32[2,1,64,640]{3,2,1,0:T(8,128)S(1)} all-gather(f32[2,1,32,640]{3,2,1,0:T(8,128)S(1)} %get-tuple-element.22), channel_id=3, replica_groups=mesh['leaf'=16,'face'=2] {'face'}, dimensions={2}, use_global_device_ids=true | all-gather | bytes 491520 | tf_op jit(solution)/shard_map/all_gather | solution.py:85
  54.3 1.5 %collective-permute-start.1 = (f32[2,64,640]{2,1,0:T(8,128)S(1)}, f32[2,64,640]{2,1,0:T(8,128)S(1)}, u32[]{:S(2)}, u32[]{:S(2)}) collective-permute-start(f32[2,64,640]{2,1,0:T(8,128)S(1)} %bitcast.97), channel_id=1, source_target_pairs={{0,2},{2,0},{4,6},{6,4},{8,10},{10,8},{12,14},{14,12},{16,18},{18,... | collective-permute-start | bytes 983048 | tf_op jit(solution)/shard_map/ppermute | solution.py:8
  55.8 2.2 %maximum_select_fusion = f32[2,4,32,10,64]{4,3,2,1,0:T(8,128)S(1)} fusion(f32[2,2,32,10,64]{4,3,2,1,0:T(8,128)} %concatenate.82, f32[2,2,32,10,64]{4,3,2,1,0:T(8,128)S(1)} %concatenate.81, f32[2,3,32,10,64]{4,3,2,1,0:T(8,128)} %concatenate.85, f32[2,1,32,10,64]{4,3,2,1,0:T(8,128)} %bitcast.92, pred[]{:T(512)S(6)} %eq.31), kind=kLoop, calls=%fused_computation | loop fusion | flops 491520 | bytes 1966081 | tf_op jit(solution)/shard_map/jit(_where)/select_n | solution.py:98
  58.0 1.3 fusion.16
  59.2 4.0 %collective-permute-done.1 = f32[2,64,640]{2,1,0:T(8,128)S(1)} collective-permute-done((f32[2,64,640]{2,1,0:T(8,128)S(1)}, f32[2,64,640]{2,1,0:T(8,128)S(1)}, u32[]{:S(2)}, u32[]{:S(2)}) %collective-permute-start.1) | collective-permute-done | bytes 327712 | tf_op jit(solution)/shard_map/ppermute | solution.py:8
  63.3 1.1 copy.31
  64.4 1.5 %collective-permute-start.2 = (f32[2,128,10,64]{1,3,2,0:T(8,128)}, f32[2,128,10,64]{1,3,2,0:T(8,128)S(1)}, u32[]{:S(2)}, u32[]{:S(2)}) collective-permute-start(f32[2,128,10,64]{1,3,2,0:T(8,128)} %bitcast.89), channel_id=1, source_target_pairs={{0,4},{2,6},{4,0},{6,2},{8,12},{10,14},{12,8},{14,10},{16,20},{18,... | collective-permute-start | bytes 1966088 | tf_op jit(solution)/shard_map/ppermute | solution.py:8
  66.5 0.9 maximum_select_fusion.1
  68.3 1.6 %maximum_select_fusion.2 = f32[2,4,32,2,64]{4,3,2,1,0:T(2,128)S(1)} fusion(f32[2,4,32,1,64]{4,3,2,1,0:T(1,128)} %get-tuple-element.8, f32[2,4,32,1,64]{4,3,2,1,0:T(1,128)} %get-tuple-element.9, f32[2,4,32,1,64]{4,3,2,1,0:T(1,128)S(1)} %get-tuple-element.6, f32[2,4,32,1,64]{4,3,2,1,0:T(1,128)S(1)} %copy-done.4, pred[]{:T(512)S(6)} %eq.31), kind=kLoop, calls=%fused_computation.24 | loop fusion | flops 98304 | bytes 393217 | tf_op jit(solution)/shard_map/jit(_where)/select_n | solution.py:104
  70.1 9.6 %collective-permute-done.2 = f32[2,128,10,64]{1,3,2,0:T(8,128)S(1)} collective-permute-done((f32[2,128,10,64]{1,3,2,0:T(8,128)}, f32[2,128,10,64]{1,3,2,0:T(8,128)S(1)}, u32[]{:S(2)}, u32[]{:S(2)}) %collective-permute-start.2) | collective-permute-done | bytes 655392 | tf_op jit(solution)/shard_map/ppermute | solution.py:8
  80.5 23.5 %custom-call.24 = f32[2,128,128]{2,1,0:T(8,128)S(1)} custom-call(f32[2,128,128]{2,1,0:T(8,128)S(1)} %fusion.8), custom_call_target="Cholesky" | custom-call | tf_op jit(solution)/shard_map/jit(cholesky)/cholesky | solution.py:13
  104.3 19.7 %custom-call.25 = f32[2,1,128,128]{2,3,1,0:T(8,128)S(1)} custom-call(f32[2,1,128,128]{3,2,1,0:T(8,128)S(1)} %select_bitcast_fusion), custom_call_target="InvertDiagBlocksLowerTriangular" | custom-call | tf_op jit(solution)/shard_map/jit(_cho_solve)/vmap()/triangular_solve | solution.py:15
  124.4 1.0 fusion.1
  125.4 1.1 fusion.6
  126.5 1.0 convolution_bitcast_fusion
  127.5 2.0 %fusion = f32[2,4,1,32,1024]{4,3,2,1,0:T(8,128)} fusion(f32[2,4,32,128]{3,2,1,0:T(8,128)S(1)} %select_n.183, f32[2,128,1024,1]{2,1,3,0:T(8,128)S(1)} %convolution_bitcast_fusion, f32[2,4,32,512]{3,2,1,0:T(8,128)S(1)} %select_n.179, pred[]{:T(512)S(6)} %eq.31), kind=kOutput, calls=%fused_computation.3 | convolution fusion | flops 403177472 | bytes 2752513 | tf_op jit(solution)/shard_map/lfhk,lkc->lfhc/dot_general | solution.py:112
  (70 shorter events, 9.1 us)
Async XLA Ops:
  0.0 1.7 %copy-start = (bf16[2,216,384]{2,1,0:T(8,128)(2,1)S(1)}, bf16[2,216,384]{2,1,0:T(8,128)(2,1)}, u32[]{:S(2)}) copy-start(bf16[2,216,384]{2,1,0:T(8,128)(2,1)} %param.6) | copy-start | bytes 995332
  2.8 0.7 copy-start.5
  6.1 14.4 %collective-permute-start = (f32[2,64,6,64]{3,2,1,0:T(8,128)S(1)}, f32[2,64,6,64]{3,2,1,0:T(8,128)}, u32[]{:S(2)}, u32[]{:S(2)}) collective-permute-start(f32[2,64,6,64]{3,2,1,0:T(8,128)S(1)} %bitcast.91), channel_id=1, source_target_pairs={{0,2},{2,0},{4,6},{6,4},{8,10},{10,8},{12,14},{14,12},{16,18},{18,... | collective-permute-start | bytes 589832 | tf_op jit(solution)/shard_map/ppermute | solution.py:8
  44.9 1.9 %copy-start.2 = (f32[2,5,32,320]{3,2,1,0:T(8,128)S(1)}, f32[2,5,32,320]{3,2,1,0:T(8,128)}, u32[]{:S(2)}) copy-start(f32[2,5,32,320]{3,2,1,0:T(8,128)} %reshape.99) | copy-start | bytes 1228804
  44.9 1.9 %copy-start.3 = (f32[2,5,32,1,64]{4,3,2,1,0:T(1,128)S(1)}, f32[2,5,32,1,64]{4,3,2,1,0:T(1,128)}, u32[]{:S(2)}) copy-start(f32[2,5,32,1,64]{4,3,2,1,0:T(1,128)} %get-tuple-element.19) | copy-start | bytes 245764
  54.3 8.9 %collective-permute-start.1 = (f32[2,64,640]{2,1,0:T(8,128)S(1)}, f32[2,64,640]{2,1,0:T(8,128)S(1)}, u32[]{:S(2)}, u32[]{:S(2)}) collective-permute-start(f32[2,64,640]{2,1,0:T(8,128)S(1)} %bitcast.97), channel_id=1, source_target_pairs={{0,2},{2,0},{4,6},{6,4},{8,10},{10,8},{12,14},{14,12},{16,18},{18,... | collective-permute-start | bytes 983048 | tf_op jit(solution)/shard_map/ppermute | solution.py:8
  64.4 15.3 %collective-permute-start.2 = (f32[2,128,10,64]{1,3,2,0:T(8,128)}, f32[2,128,10,64]{1,3,2,0:T(8,128)S(1)}, u32[]{:S(2)}, u32[]{:S(2)}) collective-permute-start(f32[2,128,10,64]{1,3,2,0:T(8,128)} %bitcast.89), channel_id=1, source_target_pairs={{0,4},{2,6},{4,0},{6,2},{8,12},{10,14},{12,8},{14,10},{16,20},{18,... | collective-permute-start | bytes 1966088 | tf_op jit(solution)/shard_map/ppermute | solution.py:8
  67.4 0.9 copy-start.4
  67.4 12.3 %copy-start.1 = (f32[2,128,640]{1,2,0:T(8,128)S(1)}, f32[2,128,640]{1,2,0:T(8,128)}, u32[]{:S(2)}) copy-start(f32[2,128,640]{1,2,0:T(8,128)} %copy.31) | copy-start | bytes 1966084
where the time goes:
time: 132 us; the launch traced here: 130 us
  other arithmetic  76.2 us (58%)
  waiting for transfers between devices  20.7 us (16%)
  local copies, waits for them, and re-layouts  12.4 us (9%)
  matrix products  9.5 us (7%)
  starting transfers between devices  5.29 us (4%)
  blocking collectives  4.91 us (4%)
    another operation x8, other arithmetic, solve_block(): factor = jnp.linalg.cholesky(normal)  35.5 us
    another operation x6, other arithmetic, solve_block(): return jax.scipy.linalg.cho_solve((factor, True), projected)  29.7 us
    ppermute x3, waiting for transfers between devices, from_partner(): lax.ppermute(shard, axis, [(i, i ^ 1 << apart) for i in range(lax.axis_si...  20.7 us
    ppermute x3, starting transfers between devices, from_partner(): lax.ppermute(shard, axis, [(i, i ^ 1 << apart) for i in range(lax.axis_si...  5.29 us
    concatenate x4, local copies, waits for them, and re-layouts, pick_blocks(): jnp.concatenate([lax.slice_in_dim(values, index, index + 1, axis=axis) fo...  3.82 us
    slice x15, local copies, waits for them, and re-layouts, pick_blocks(): lax.slice_in_dim(values, index, index + 1, axis=axis)  3.3 us
    another operation x4, matrix products, solve_block(): return jax.scipy.linalg.cho_solve((factor, True), projected)  2.93 us
    all_gather x1, blocking collectives, local(): box_local = lax.all_gather(box_face, 'face', axis=1, tiled=True)  2.73 us
  transfers between devices with their start and end apart: 3, of which 3 were waited for; matrix products, arithmetic and copies ran while one was open for 9% of the time, Pallas kernels for 0%

commit v1 on v0

v1 whole, which is shorter than its diff:
```python
import functools

import jax
import jax.numpy as jnp
from jax import lax
from jax.experimental import pallas as pl
from jax.experimental.pallas import tpu as pltpu
from jax.sharding import PartitionSpec as P

MESH = pl.DeviceIdType.MESH
F32 = jnp.float32
BF16 = jnp.bfloat16
LIMIT = 60


def lanes_of(shape):
    return lax.broadcasted_iota(jnp.int32, shape, len(shape) - 1)


def turn(x):
    return pltpu.roll(x, 64, 1)


def leaf_rows(values, diag, stencil, weights, faces, core, s, q):
    half = 32
    lane = lanes_of((half, 128))
    row = lax.broadcasted_iota(jnp.int32, (half, 128), 0)
    tiles = []
    for n, face in enumerate(faces):
        part = values[n * half : (n + 1) * half]
        side = face % 2
        spot = lane - side * 64
        extra = jnp.where(spot == core * half + row, diag[n], 0.0)
        on = jnp.logical_and(spot >= 0, spot < 64)
        extra = extra + jnp.where(on, stencil * weights[n], 0.0)
        tiles.append(
            [part[:, t * 128 : t * 128 + 128] + jnp.where(face // 2 == t, extra, 0.0) for t in range(3)]
        )
    xt, yt, zt = (jnp.concatenate([row_tiles[t] for row_tiles in tiles], axis=0) for t in range(3))
    left = lanes_of(xt.shape) < 64
    xr, yr = turn(xt), turn(yt)
    first, lower = s == 0, q == 0
    outer = jnp.where(left, jnp.where(first, xt, xr), jnp.where(lower, yr, yt))
    inner = jnp.where(left, jnp.where(first, xr, xt), jnp.where(lower, yt, yr))
    return outer, zt, inner


def gather_kernel(solve, deriv, diag, stencil, coef, cut, g, own, send, recv):
    me = lax.axis_index("leaf")
    core = lax.axis_index("face")
    s, q = me % 2, me // 2 % 2
    xdev = (me + 1 - 2 * s, core)
    ydev = (me + 2 - 4 * q, core)
    cdev = (me, 1 - core)
    barrier = pltpu.get_barrier_semaphore()
    for dev in (xdev, ydev, cdev):
        pl.semaphore_signal(barrier, inc=1, device_id=dev, device_id_type=MESH)

    rows = pl.ds(pl.multiple_of(core * 32, 32), 32)

    def copy(index, qq, ss, l, dev):
        where = g.at[qq, ss, l, :, rows, :]
        return pltpu.make_async_remote_copy(
            src_ref=where, dst_ref=where, send_sem=send.at[index], recv_sem=recv.at[index],
            device_id=dev, device_id_type=MESH,
        )

    st = stencil[0]
    st = jnp.concatenate([st, st], axis=1)

    def compute(l, faces):
        d = jnp.concatenate([deriv[f, 0] for f in faces], axis=0)
        values = jnp.dot(d, solve[l], preferred_element_type=F32)
        dd = [jnp.concatenate([diag[f]] * 4, axis=1) for f in faces]
        w = [cut[l, f].astype(F32) * coef[l, f] for f in faces]
        return leaf_rows(values, dd, st, w, faces, core, s, q)

    shared = (1 - s, 3 - q)
    for l in range(2):
        for t, tile in enumerate(compute(l, shared)):
            g[q, s, l, 0, rows, t * 128 : t * 128 + 128] = tile[:32]
            g[q, s, l, 1, rows, t * 128 : t * 128 + 128] = tile[32:]
    pl.semaphore_wait(barrier, 3)
    x0, y1 = copy(0, q, s, 0, xdev), copy(1, q, s, 1, ydev)
    x1, y0 = copy(2, q, s, 1, xdev), copy(3, q, s, 0, ydev)
    c0, c1 = copy(4, q, s, 0, cdev), copy(5, q, s, 1, cdev)
    started = [x0, y1, x1, y0, c0, c1]
    for one in started:
        one.start()
    kept = (s, 2 + q, 4, 5)
    for l in range(2):
        for t, tile in enumerate(compute(l, kept)):
            own[l, :, t * 128 : t * 128 + 128] = tile
    later = [
        (x0, [(6, q, 1 - s, 0, ydev), (7, q, 1 - s, 0, cdev)]),
        (y1, [(8, 1 - q, s, 1, xdev), (9, 1 - q, s, 1, cdev)]),
        (x1, [(10, q, 1 - s, 1, cdev)]),
        (y0, [(11, 1 - q, s, 0, cdev)]),
    ]
    done = {}
    for first, relays in later:
        first.wait_recv()
        for relay in relays:
            done[relay[0]] = copy(*relay)
            done[relay[0]].start()
    done[6].wait_recv()
    done[12] = copy(12, 1 - q, 1 - s, 0, cdev)
    done[12].start()
    done[8].wait_recv()
    done[13] = copy(13, 1 - q, 1 - s, 1, cdev)
    done[13].start()
    c0.wait_recv()
    c1.wait_recv()
    for index in (7, 9, 10, 11, 12, 13):
        done[index].wait_recv()
    for one in started + list(done.values()):
        one.wait_send()


def split(x):
    hi = x.astype(BF16)
    return hi, (x - hi.astype(F32)).astype(BF16)


def dot(a, b):
    return jnp.dot(a, b, preferred_element_type=F32)


def mul(a, b):
    ah, al = split(a)
    bh, bl = split(b)
    both = jnp.concatenate([ah, al], axis=1)
    if b.shape[1] == 128:
        weights = jnp.concatenate(
            [jnp.concatenate([bh, bl], axis=1), jnp.concatenate([bh, jnp.zeros_like(bl)], axis=1)], axis=0
        )
        out = dot(both, weights)
        return out[:, :128] + out[:, 128:]
    return dot(both, jnp.concatenate([bh, bh], axis=0)) + dot(ah, bl)


def invert(mats):
    row = lax.broadcasted_iota(jnp.int32, (128, 128), 0)
    eye = (row == lanes_of((128, 128))).astype(F32)
    state = []
    for m in mats:
        mt = m.T
        gram = mul(m, mt)
        scale = 1.9 / jnp.max(jnp.sum(jnp.abs(gram), axis=1, keepdims=True), axis=0, keepdims=True)
        state += [mt * scale, eye - gram * scale]

    def size(st):
        worst = jnp.maximum(jnp.abs(st[1]), jnp.abs(st[3]))
        return jnp.max(worst)

    def step(st):
        out = []
        for x, r in ((st[0], st[1]), (st[2], st[3])):
            both = mul(jnp.concatenate([x, r], axis=0), r)
            out += [x + both[:128], both[128:]]
        return out

    def body(carry):
        st = list(carry[2:])
        st = step(st)
        return (carry[0] + 1, size(st), *st)

    st = state
    for _ in range(6):
        st = step(st)
    final = lax.while_loop(
        lambda c: jnp.logical_and(c[0] < LIMIT, c[1] > 1e-4), body, (jnp.int32(0), size(st), *st)
    )
    out = []
    for m, x in zip(mats, (final[2], final[4])):
        out.append(x + mul(x, eye - mul(m, x)))
    return out


def merge_kernel(g, own, out):
    me = lax.axis_index("leaf")
    s, q = me % 2, me // 2 % 2
    left64 = lanes_of((64, 128)) < 64
    left128 = lanes_of((128, 128)) < 64
    pairs = (q, 1 - q)
    zero = jnp.zeros((64, 128), F32)
    mats = []
    for p in pairs:
        sums = [g[p, 0, l, 0, :, 256:384] + g[p, 1, l, 0, :, 256:384] for l in range(2)]
        mats.append(
            jnp.concatenate(
                [jnp.where(left64, sums[0], zero), jnp.where(left64, zero, turn(sums[1]))], axis=0
            )
        )
    inverses = invert(mats)
    weights = []
    for p, inverse, extra in zip(pairs, inverses, (True, False)):
        rows = [
            jnp.where(left64, g[p, e, 0, 1, :, 256:384], turn(g[p, e, 1, 1, :, 256:384])) for e in range(2)
        ]
        if extra:
            rows.append(jnp.where(left128, own[0, :, 256:384], turn(own[1, :, 256:384])))
        weights.append(mul(jnp.concatenate(rows, axis=0), inverse))

    schur, coupled, keep_outer, keep_inner = [], [], [], []
    for l in range(2):
        inner_tiles, outer_parts = [], []
        for p, w, extra in zip(pairs, weights, (True, False)):
            wl = w if l == 0 else turn(w)
            left = lanes_of(wl.shape) < 64
            hi = wl.astype(BF16).astype(F32)
            lo = wl - hi
            lhs = jnp.concatenate(
                [jnp.where(left, hi, turn(lo)).astype(BF16), jnp.where(left, hi, 0.0).astype(BF16)], axis=1
            )
            joint = jnp.where(left64, turn(g[p, 0, l, 0, :, 256:384]), g[p, 1, l, 0, :, 256:384])
            right = jnp.concatenate([g[p, 0, l, 0, :, 0:256], g[p, 1, l, 0, :, 0:256], joint], axis=1)
            bh, bl = split(right)
            prod = dot(lhs, jnp.concatenate([bh, bh, bl, bl], axis=0))
            zeros = jnp.zeros((64, 256), F32)
            base = jnp.concatenate(
                [
                    jnp.concatenate(
                        [
                            g[p, 0, l, 1, :, 0:256],
                            zeros,
                            jnp.where(left64, turn(g[p, 0, l, 1, :, 256:384]), zero),
                        ],
                        axis=1,
                    ),
                    jnp.concatenate(
                        [zeros, g[p, 1, l, 1, :, 0:256], jnp.where(left64, zero, g[p, 1, l, 1, :, 256:384])],
                        axis=1,
                    ),
                ],
                axis=0,
            )
            rows = base - prod[:128]
            outer_parts.append(rows[:, :512])
            inner_tiles.append(rows[:, 512:])
            if extra:
                first = s == 0
                mine = own[l, :, 0:256]
                face = own[l, :, 256:384]
                keep_outer.append(
                    jnp.concatenate([jnp.where(first, mine, 0.0), jnp.where(first, 0.0, mine)], axis=1)
                    - prod[128:, :512]
                )
                placed = jnp.where(
                    left128, jnp.where(first, turn(face), 0.0), jnp.where(first, 0.0, face)
                )
                keep_inner.append(placed - prod[128:, 512:])
        schur.append(inner_tiles[0] + inner_tiles[1])
        coupled.append(outer_parts)
    inverses = invert(schur)
    here = pl.ds(pl.multiple_of(q * 512, 512), 512)
    there = pl.ds(pl.multiple_of((1 - q) * 512, 512), 512)
    for l in range(2):
        w = mul(keep_inner[l], inverses[l])
        out[l, :, here] = keep_outer[l] - mul(w, coupled[l][0])
        out[l, :, there] = -mul(w, coupled[l][1])


def local(solve_ops, inner_deriv, boundary_diag, wall_stencil, wall_coef, cut_faces):
    leaves, inner, bound = solve_ops.shape
    faces, _, half, _ = inner_deriv.shape
    vmem = pl.BlockSpec(memory_space=pltpu.VMEM)
    smem = pl.BlockSpec(memory_space=pltpu.SMEM)
    g, own = pl.pallas_call(
        gather_kernel,
        out_shape=(
            jax.ShapeDtypeStruct((2, 2, leaves, 2, 2 * half, bound), F32),
            jax.ShapeDtypeStruct((leaves, 4 * half, bound), F32),
        ),
        in_specs=[vmem, vmem, vmem, vmem, smem, smem],
        out_specs=(vmem, vmem),
        scratch_shapes=[pltpu.SemaphoreType.DMA((14,)), pltpu.SemaphoreType.DMA((14,))],
        compiler_params=pltpu.CompilerParams(
            collective_id=0, has_side_effects=True, vmem_limit_bytes=32 * 1024 * 1024
        ),
        name="gather_rows",
    )(solve_ops, inner_deriv, boundary_diag, wall_stencil, wall_coef, cut_faces)
    merged = pl.pallas_call(
        merge_kernel,
        out_shape=jax.ShapeDtypeStruct((leaves, 4 * half, 16 * 2 * half), F32),
        in_specs=[vmem, vmem],
        out_specs=vmem,
        compiler_params=pltpu.CompilerParams(vmem_limit_bytes=48 * 1024 * 1024),
        name="merge_levels",
    )(g, own)
    return merged.reshape(leaves, 4, 1, half, 16 * 2 * half)


def solution(mesh):
    in_specs = (
        P("leaf", None, None),
        P(None, "face", None, None),
        P(None, "face", None),
        P("face", None, None),
        P("leaf", None),
        P("leaf", None),
    )
    out_specs = P("leaf", None, "face", None, None)
    return jax.shard_map(local, mesh=mesh, in_specs=in_specs, out_specs=out_specs, check_vma=False)
```

time: 132 us -> 26.6 us (0.20); the launches traced: 130 us -> 26.3 us
  other arithmetic: 76.2 us -> 0 us
  Pallas kernels: 0 us -> 21.6 us
  waiting for transfers between devices: 20.7 us -> 0 us
  matrix products: 9.5 us -> 0 us
  local copies, waits for them, and re-layouts: 12.4 us -> 4.62 us
  starting transfers between devices: 5.29 us -> 0 us
  blocking collectives: 4.91 us -> 0 us
    another operation x16 -> x0, other arithmetic: 65.3 us -> none  [the longest x8 35.5 us: solve_block(): factor = jnp.linalg.cholesky(normal)]
    pallas_call x0 -> x2, Pallas kernels: none -> 21.6 us  [the longest x1 13 us: local(): pl.pallas_call(gather_kernel, out_shape=(jax.ShapeDtypeStruct((2, 2, leav...]
    ppermute x3 -> x0, waiting for transfers between devices: 20.7 us -> none  [from_partner(): lax.ppermute(shard, axis, [(i, i ^ 1 << apart) for i in range(lax.axis_si...]
    select_n x10 -> x0, other arithmetic: 7.88 us -> none  [the longest x1 2.2 us: local(): jnp.where(lower, pick_blocks(level_one, (0, 1, 3, 4), 1), pick_blocks(lev...]
    dot_general x7 -> x0, matrix products: 6.57 us -> none  [the longest x1 2 us: local(): jnp.einsum('lfhk,lkc->lfhc', keep_inner, solved_two, precision=lax.Precis...]
    ppermute x3 -> x0, starting transfers between devices: 5.29 us -> none  [from_partner(): lax.ppermute(shard, axis, [(i, i ^ 1 << apart) for i in range(lax.axis_si...]
    concatenate x6 -> x0, local copies, waits for them, and re-layouts: 5.23 us -> none  [the longest x4 3.82 us: pick_blocks(): jnp.concatenate([lax.slice_in_dim(values, index, index + 1, axis=axis) fo...]
    all_gather x2 -> x0, blocking collectives: 4.91 us -> none  [the longest x1 2.73 us: local(): box_local = lax.all_gather(box_face, 'face', axis=1, tiled=True)]
  transfers between devices with their start and end apart: 3 -> 0, of which waited for: 3 -> 0; matrix products, arithmetic and copies ran while one was open for 9% -> 0% of each run, Pallas kernels for 0% -> 0%
where the time goes in v1:
time: 26.6 us; the launch traced here: 26.3 us
  Pallas kernels  21.6 us (81%)
  local copies, waits for them, and re-layouts  4.62 us (17%)
    pallas_call x1, Pallas kernels, local(): pl.pallas_call(gather_kernel, out_shape=(jax.ShapeDtypeStruct((2, 2, leav...  13 us
    pallas_call x1, Pallas kernels, local(): pl.pallas_call(merge_kernel, out_shape=jax.ShapeDtypeStruct((leaves, 4 *...  8.6 us
    unnamed x12, local copies, waits for them, and re-layouts  4.62 us

profile of v1, /device:TPU:1, one launch (start us, length us, event | category | flops | bytes accessed | tf_op | source)
XLA Modules:
  0.0 26.3 jit_solution(9503654178025918825)
XLA Ops:
  0.0 0.0 copy-start
  0.0 1.0 %copy-done = bf16[2,216,384]{2,1,0:T(8,128)(2,1)S(1)} copy-done((bf16[2,216,384]{2,1,0:T(8,128)(2,1)S(1)}, bf16[2,216,384]{2,1,0:T(8,128)(2,1)}, u32[]{:S(2)}) %copy-start) | copy-done | bytes 331800
  1.0 0.0 copy-start.1
  1.0 0.9 %copy-done.1 = bf16[6,1,32,216]{3,2,1,0:T(8,128)(2,1)S(1)} copy-done((bf16[6,1,32,216]{3,2,1,0:T(8,128)(2,1)S(1)}, bf16[6,1,32,216]{3,2,1,0:T(8,128)(2,1)}, u32[]{:S(2)}) %copy-start.1) | copy-done | bytes 82968
  1.9 0.0 copy-start.2
  1.9 0.7 %copy-done.2 = f32[1,32,64]{2,1,0:T(8,128)S(1)} copy-done((f32[1,32,64]{2,1,0:T(8,128)S(1)}, f32[1,32,64]{2,1,0:T(8,128)}, u32[]{:S(2)}) %copy-start.2) | copy-done | bytes 8216
  2.6 0.0 copy-start.3
  2.6 0.7 %copy-done.3 = f32[6,1,32]{2,1,0:T(1,128)S(1)} copy-done((f32[6,1,32]{2,1,0:T(1,128)S(1)}, f32[6,1,32]{2,1,0:T(1,128)}, u32[]{:S(2)}) %copy-start.3) | copy-done | bytes 792
  3.3 0.0 copy-start.4
  3.3 0.7 %copy-done.4 = f32[2,6]{1,0:T(2,128)S(1)} copy-done((f32[2,6]{1,0:T(2,128)S(1)}, f32[2,6]{1,0:T(2,128)}, u32[]{:S(2)}) %copy-start.4) | copy-done | bytes 72
  4.0 0.0 copy-start.5
  4.0 0.7 %copy-done.5 = s32[2,6]{1,0:T(2,128)S(1)} copy-done((s32[2,6]{1,0:T(2,128)S(1)}, s32[2,6]{1,0:T(2,128)}, u32[]{:S(2)}) %copy-start.5) | copy-done | bytes 72
  4.6 13.0 %gather_rows.1 = (f32[2,2,2,2,64,384]{5,4,3,2,1,0:T(8,128)S(1)}, f32[2,128,384]{2,1,0:T(8,128)S(1)}) custom-call(bf16[2,216,384]{2,1,0:T(8,128)(2,1)S(1)} %copy-done, bf16[6,1,32,216]{3,2,1,0:T(8,128)(2,1)S(1)} %copy-done.1, f32[6,1,32]{2,1,0:T(1,128)S(1)} %copy-done.3, f32[1,32,64]{2,1,0:T(8,128)S(1)} %copy-done.2, f32[2,6]{1,0:T(2,128)S(1)} %copy-done.4, ...), custom_call_target="tpu_custom_call" | custom-call | tf_op jit(solution)/shard_map/gather_rows/pallas_call | solution.py:269
  17.7 8.6 %merge_levels.1 = f32[2,128,1024]{2,1,0:T(8,128)} custom-call(f32[2,2,2,2,64,384]{5,4,3,2,1,0:T(8,128)S(1)} %get-tuple-element.7.g, f32[2,128,384]{2,1,0:T(8,128)S(1)} %get-tuple-element.8.own), custom_call_target="tpu_custom_call" | custom-call | tf_op jit(solution)/shard_map/merge_levels/pallas_call | solution.py:283
Async XLA Ops:
  0.0 1.0 %copy-start = (bf16[2,216,384]{2,1,0:T(8,128)(2,1)S(1)}, bf16[2,216,384]{2,1,0:T(8,128)(2,1)}, u32[]{:S(2)}) copy-start(bf16[2,216,384]{2,1,0:T(8,128)(2,1)} %solve.1) | copy-start | bytes 995332
  1.0 0.9 %copy-start.1 = (bf16[6,1,32,216]{3,2,1,0:T(8,128)(2,1)S(1)}, bf16[6,1,32,216]{3,2,1,0:T(8,128)(2,1)}, u32[]{:S(2)}) copy-start(bf16[6,1,32,216]{3,2,1,0:T(8,128)(2,1)} %deriv.1) | copy-start | bytes 248836
  1.9 0.7 %copy-start.2 = (f32[1,32,64]{2,1,0:T(8,128)S(1)}, f32[1,32,64]{2,1,0:T(8,128)}, u32[]{:S(2)}) copy-start(f32[1,32,64]{2,1,0:T(8,128)} %stencil.1) | copy-start | bytes 24580
  2.6 0.7 %copy-start.3 = (f32[6,1,32]{2,1,0:T(1,128)S(1)}, f32[6,1,32]{2,1,0:T(1,128)}, u32[]{:S(2)}) copy-start(f32[6,1,32]{2,1,0:T(1,128)} %diag.1) | copy-start | bytes 2308
  3.3 0.7 %copy-start.4 = (f32[2,6]{1,0:T(2,128)S(1)}, f32[2,6]{1,0:T(2,128)}, u32[]{:S(2)}) copy-start(f32[2,6]{1,0:T(2,128)} %coef.1) | copy-start | bytes 148
  4.0 0.7 %copy-start.5 = (s32[2,6]{1,0:T(2,128)S(1)}, s32[2,6]{1,0:T(2,128)}, u32[]{:S(2)}) copy-start(s32[2,6]{1,0:T(2,128)} %cut.1) | copy-start | bytes 148
